TPU v7x, 32 devices: a whole 2x2x4 slice. The times are simulated.
32 devices in a mesh: lon: 4 (over z), lat: 2 (over x), mem: 4 (over y, core).
Axes of the slice: x: 2, y: 2, z: 4, core: 2. Of those that a mesh axis runs over, the one named last changes fastest.
Arguments:
- perturb: float32 [8, 2, 2048, 1024], P('mem', None, 'lat', 'lon'), may hold values from -6 to 6
- control: float32 [8, 2, 2048, 1024], P('mem', None, 'lat', 'lon'), may hold values from -6 to 6
- diffusivity: float32 [2048, 1024], P('lat', 'lon'), may hold values from 0.05 to 0.24
- sea_mask: int32 [2, 2048, 1024], P(None, 'lat', 'lon'), may hold values 0 or 1
- fold_partner: int32 [1024], replicated, may hold values from 0 to 1023, as said below
Outputs:
- increment: float32 [2, 2048, 1024], P(None, 'lat', 'lon')
Inputs may be any that keep to these rules, and one draw needn't show every extreme that they name: `sea_mask`: 1 marks sea and 0 land. fold_partner[i] = (2 p - 1 - i) mod 1024 for a fold pivot column p of the case; it is its own inverse and never maps a column to itself.
All inputs are finite; a program needn't handle non-finite values. No bound on the sum of `sea_mask` on one device may be relied on, other than what follows from the above.
Results may differ from a plain program's by a relative error of at most 0.00002.
Values sent between devices are 32-bit elements; how exact they have to be, the bound alone decides.
A program may use at most 192 MiB of HBM per device.

v0:
```python
import functools
import jax
import jax.numpy as jnp
from jax import lax
from jax.experimental import pallas as pl
from jax.experimental.pallas import tpu as pltpu
from jax.sharding import PartitionSpec as P

PASSES = 3
CHUNK = 128
PIECE = 256
MESH = pl.DeviceIdType.MESH


def kernel(
    control, perturb, kappa, sea, side_f, side_i, rim_f, rim_i, out,
    field, weight, kap, mask, g_east, g_north, state,
    part, part_in, pair, pair_in, total,
    in_sem, halo_sem, a_send, a_recv, b_send, b_recv, c_send, c_recv, o_sem,
):
    rows = control.shape[1]
    cols = control.shape[2]
    wide = cols + 128
    blocks = rows // 8
    chunks = rows // CHUNK
    pieces = rows // PIECE
    per_chunk = CHUNK // 8
    mem = lax.axis_index("mem")
    core = lax.rem(mem, 2)
    twin = {"mem": mem + 1 - 2 * core}
    across = {"mem": lax.rem(mem + 2, 4)}

    def piece_copies(p):
        src = pl.ds(pl.multiple_of(p * PIECE, PIECE), PIECE)
        dst = pl.ds(pl.multiple_of(p * PIECE + 8, 8), PIECE)
        return (
            pltpu.make_async_copy(kappa.at[src], kap.at[dst, 0:cols], in_sem.at[0, p]),
            pltpu.make_async_copy(sea.at[:, src], mask.at[:, dst, 0:cols], in_sem.at[1, p]),
            pltpu.make_async_copy(control.at[:, src], field.at[:, dst, 0:cols], in_sem.at[2, p]),
            pltpu.make_async_copy(perturb.at[:, src], weight.at[:, src], in_sem.at[3, p]),
        )

    low = pl.ds(0, 8)
    high = pl.ds(rows + 8, 8)
    main = pl.ds(0, cols)
    side = pl.ds(cols, 128)
    halo_copies = [
        pltpu.make_async_copy(side_f.at[0:4], field.at[:, :, side], halo_sem.at[0]),
        pltpu.make_async_copy(side_f.at[4], kap.at[:, side], halo_sem.at[1]),
        pltpu.make_async_copy(side_i, mask.at[:, :, side], halo_sem.at[2]),
        pltpu.make_async_copy(rim_f.at[0, 0:4], field.at[:, low, main], halo_sem.at[3]),
        pltpu.make_async_copy(rim_f.at[0, 4], kap.at[low, main], halo_sem.at[4]),
        pltpu.make_async_copy(rim_i.at[0], mask.at[:, low, main], halo_sem.at[5]),
        pltpu.make_async_copy(rim_f.at[1, 0:4], field.at[:, high, main], halo_sem.at[6]),
        pltpu.make_async_copy(rim_f.at[1, 4], kap.at[high, main], halo_sem.at[7]),
        pltpu.make_async_copy(rim_i.at[1], mask.at[:, high, main], halo_sem.at[8]),
    ]
    for copy in halo_copies:
        copy.start()
    for copy in piece_copies(0):
        copy.start()

    barrier = pltpu.get_barrier_semaphore()
    for peer in (twin, across):
        pl.semaphore_signal(barrier, inc=1, device_id=peer, device_id_type=MESH)
    pl.semaphore_wait(barrier, 2)

    for p in range(1, pieces):
        for copy in piece_copies(p):
            copy.start()
    for copy in halo_copies:
        copy.wait()
    for copy in piece_copies(0):
        copy.wait()

    row_id = lax.broadcasted_iota(jnp.int32, (8, wide), 0)
    first = row_id == 0
    last = row_id == 7

    def block(idx):
        return pl.ds(pl.multiple_of(idx * 8, 8), 8)

    def apply(cur, nxt, flux_before, ge, gn):
        north = gn * (pltpu.roll(jnp.where(first, nxt, cur), 7, 0) - cur)
        south = pltpu.roll(jnp.where(last, flux_before, north), 1, 0)
        east = ge * (pltpu.roll(cur, wide - 1, 1) - cur)
        west = pltpu.roll(east, 1, 1)
        return cur + ((east - west) + (north - south)), north

    def step(o, carry, level):
        here = jnp.minimum(o + 5, blocks + 1)
        ahead = jnp.minimum(o + 6, blocks + 1)
        second = jnp.minimum(jnp.maximum(o + 3, 0), blocks + 1)
        third = jnp.maximum(o + 1, 0)
        k_here = kap[block(here)]
        s_here = mask[level, block(here)].astype(jnp.float32)
        k_ahead = kap[block(ahead)]
        s_ahead = mask[level, block(ahead)].astype(jnp.float32)
        k_north = pltpu.roll(jnp.where(first, k_ahead, k_here), 7, 0)
        s_north = pltpu.roll(jnp.where(first, s_ahead, s_here), 7, 0)
        k_east = pltpu.roll(k_here, wide - 1, 1)
        s_east = pltpu.roll(s_here, wide - 1, 1)
        half = 0.5 * s_here
        gn1 = (k_here + k_north) * (half * s_north)
        ge1 = (k_here + k_east) * (half * s_east)
        g_north[level, block(here)] = gn1
        g_east[level, block(here)] = ge1
        gn2 = g_north[level, block(second)]
        ge2 = g_east[level, block(second)]
        gn3 = g_north[level, block(third)]
        ge3 = g_east[level, block(third)]
        after = []
        results = []
        for member in range(2):
            v0, f1, n1, c1, f2, n2, c2, f3 = carry[8 * member : 8 * member + 8]
            nxt = field[2 * member + level, block(ahead)]
            w1, f1 = apply(v0, nxt, f1, ge1, gn1)
            w2, f2 = apply(c1, n1, f2, ge2, gn2)
            w3, f3 = apply(c2, n2, f3, ge3, gn3)
            after += [nxt, f1, w1, n1, f2, w2, n2, f3]
            results.append(w3)
        return tuple(after), results

    for level in range(2):
        state[level] = jnp.zeros((16, 8, wide), jnp.float32)
        for member in range(2):
            state[level, 8 * member] = field[2 * member + level, 0:8]
        start = [state[level, i] for i in range(16)]
        warm = lax.fori_loop(-5, 0, lambda o, c: step(o, c, level)[0], tuple(start))
        for i, value in enumerate(warm):
            state[level, i] = value

    def diffuse_chunk(k, level, into):
        def body(j, carry):
            o = k * per_chunk + j
            carry, results = step(o, carry, level)
            acc = weight[level, block(o)] * results[0][:, 0:cols]
            acc = acc + weight[2 + level, block(o)] * results[1][:, 0:cols]
            into[k, block(j)] = acc
            return carry

        carry = tuple(state[level, i] for i in range(16))
        carry = lax.fori_loop(0, per_chunk, body, carry)
        for i, value in enumerate(carry):
            state[level, i] = value

    def send_part(k):
        return pltpu.make_async_remote_copy(
            src_ref=part.at[k], dst_ref=part_in.at[k], send_sem=a_send.at[k],
            recv_sem=a_recv.at[k], device_id=twin, device_id_type=MESH,
        )

    def send_pair(k):
        return pltpu.make_async_remote_copy(
            src_ref=pair.at[k], dst_ref=pair_in.at[k], send_sem=b_send.at[k],
            recv_sem=b_recv.at[k], device_id=across, device_id_type=MESH,
        )

    def chunk_rows(k):
        return pl.ds(pl.multiple_of(k * CHUNK, CHUNK), CHUNK)

    def send_total(k):
        return pltpu.make_async_remote_copy(
            src_ref=total.at[k], dst_ref=out.at[core, chunk_rows(k)], send_sem=c_send.at[k],
            recv_sem=c_recv.at[k], device_id=twin, device_id_type=MESH,
        )

    def store_total(k):
        return pltpu.make_async_copy(total.at[k], out.at[core, chunk_rows(k)], o_sem.at[k])

    ratio = PIECE // CHUNK

    @pl.loop(0, chunks)
    def _(k):
        @pl.when(jnp.logical_and(lax.rem(k, ratio) == ratio - 1, k < chunks - 1))
        def _():
            for copy in piece_copies(lax.div(k, ratio) + 1):
                copy.wait()

        diffuse_chunk(k, 1 - core, part)
        send_part(k).start()
        diffuse_chunk(k, core, pair)
        send_part(k).wait_recv()

        @pl.loop(0, per_chunk)
        def _(j):
            pair[k, block(j)] = pair[k, block(j)] + part_in[k, block(j)]

        send_pair(k).start()

    @pl.loop(0, chunks)
    def _(k):
        send_pair(k).wait_recv()

        @pl.loop(0, per_chunk)
        def _(j):
            sea_here = mask[core, block(k * per_chunk + j + 1), 0:cols].astype(jnp.float32)
            total[k, block(j)] = (pair[k, block(j)] + pair_in[k, block(j)]) * sea_here

        send_total(k).start()
        store_total(k).start()

    @pl.loop(0, chunks)
    def _(k):
        send_part(k).wait_send()
        send_pair(k).wait_send()
        send_total(k).wait()
        store_total(k).wait()


def shifted(block, axis, by):
    count = lax.axis_size(axis)
    return lax.ppermute(block, axis, [(i, (i + by) % count) for i in range(count)])


def per_device(perturb, control, diffusivity, sea_mask, fold_partner):
    members, levels, rows, cols = control.shape
    fields = members * levels
    flat = control.reshape(fields, rows, cols)
    sea_float = lambda s: s.astype(jnp.float32)
    lon = lax.axis_index("lon")
    lat = lax.axis_index("lat")
    top_band = lat == lax.axis_size("lat") - 1
    bottom_band = lat == 0

    def cut(r, c):
        return jnp.concatenate(
            [flat[:, r, c], diffusivity[None, r, c], sea_float(sea_mask[:, r, c])], axis=0
        )

    every = slice(None)
    north_edge = cut(slice(rows - PASSES, rows), every)
    south_edge = cut(slice(0, PASSES), every)
    from_north = shifted(south_edge, "lat", -1)
    from_south = shifted(north_edge, "lat", 1)
    gathered = lax.all_gather(north_edge, "lon", axis=2, tiled=True)
    count = gathered.shape[-1]
    flipped = gathered[:, ::-1, ::-1]
    twice = jnp.concatenate([flipped, flipped], axis=-1)
    begin = jnp.mod(count - 1 - fold_partner[0] + lon * cols, count)
    folded = lax.dynamic_slice_in_dim(twice, begin, cols, axis=2)
    north = jnp.where(top_band, folded, from_north)
    south = jnp.where(bottom_band, jnp.zeros_like(from_south), from_south)

    def strip(c):
        tall = jnp.concatenate([south[:, :, c], cut(every, c), north[:, :, c]], axis=1)
        return jnp.swapaxes(tall, 1, 2)

    from_east = shifted(strip(slice(0, PASSES)), "lon", -1)
    from_west = shifted(strip(slice(cols - PASSES, cols)), "lon", 1)
    gap = 128 - 2 * PASSES
    middle = jnp.zeros((fields + 3, gap, rows + 2 * PASSES), jnp.float32)
    side = jnp.swapaxes(jnp.concatenate([from_east, middle, from_west], axis=1), 1, 2)
    fill = 8 - PASSES
    side = jnp.pad(side, ((0, 0), (fill, fill), (0, 0)))
    rim = jnp.stack(
        [
            jnp.pad(south, ((0, 0), (fill, 0), (0, 0))),
            jnp.pad(north, ((0, 0), (0, fill), (0, 0))),
        ]
    )
    chunks = rows // CHUNK
    wide = cols + 128
    any_spec = pl.BlockSpec(memory_space=pl.ANY)
    f32 = jnp.float32
    chunk_buf = pltpu.VMEM((chunks, CHUNK, cols), f32)
    dma = pltpu.SemaphoreType.DMA
    return pl.pallas_call(
        kernel,
        out_shape=jax.ShapeDtypeStruct((levels, rows, cols), f32),
        in_specs=[any_spec] * 8,
        out_specs=any_spec,
        scratch_shapes=[
            pltpu.VMEM((fields, rows + 16, wide), f32),
            pltpu.VMEM((fields, rows, cols), f32),
            pltpu.VMEM((rows + 16, wide), f32),
            pltpu.VMEM((levels, rows + 16, wide), jnp.int32),
            pltpu.VMEM((levels, rows + 16, wide), f32),
            pltpu.VMEM((levels, rows + 16, wide), f32),
            pltpu.VMEM((levels, 16, 8, wide), f32),
            chunk_buf, chunk_buf, chunk_buf, chunk_buf, chunk_buf,
            dma((4, rows // PIECE)),
            dma((9,)),
            dma((chunks,)), dma((chunks,)), dma((chunks,)), dma((chunks,)),
            dma((chunks,)), dma((chunks,)), dma((chunks,)),
        ],
        compiler_params=pltpu.CompilerParams(
            collective_id=0, has_side_effects=True, vmem_limit_bytes=50 * 1024 * 1024
        ),
        cost_estimate=pl.CostEstimate(
            flops=40 * fields * rows * cols, bytes_accessed=16 * fields * rows * cols, transcendentals=0
        ),
    )(
        flat,
        perturb.reshape(fields, rows, cols),
        diffusivity,
        sea_mask,
        side[: fields + 1],
        side[fields + 1 :].astype(jnp.int32),
        rim[:, : fields + 1],
        rim[:, fields + 1 :].astype(jnp.int32),
    )


def solution(mesh):
    return jax.shard_map(
        per_device,
        mesh=mesh,
        in_specs=(
            P("mem", None, "lat", "lon"),
            P("mem", None, "lat", "lon"),
            P("lat", "lon"),
            P(None, "lat", "lon"),
            P(),
        ),
        out_specs=P(None, "lat", "lon"),
        check_vma=False,
    )
```

profile of v0, /device:TPU:0, one launch (start us, length us, event | category | flops | bytes accessed | tf_op | source)
XLA Modules:
  0.0 120.7 jit_solution(4188379182316535237)
XLA Ops:
  0.0 0.8 fusion.6
  0.8 0.7 slice_convert_fusion
  1.5 0.7 slice_bitcast_fusion.2
  2.3 3.0 %collective-permute-start.1 = (f32[7,3,256]{2,1,0:T(4,128)S(1)}, f32[7,3,256]{2,1,0:T(4,128)S(1)}, u32[]{:S(2)}, u32[]{:S(2)}) collective-permute-start(f32[7,3,256]{2,1,0:T(4,128)S(1)} %pad_maximum_fusion.4), channel_id=1, source_target_pairs={{0,4},{4,0},{1,5},{5,1},{2,6},{6,2},{3,7},{7,3},{8,12},{12,8},{9,1... | collective-permute-start | bytes 64520 | tf_op jit(solution)/shard_map/ppermute | solution.py:213
  5.4 1.2 slice.70
  7.2 5.0 %fusion.5 = (f32[4,1024,3]{2,1,0:T(8,128)}, f32[4,1024,3]{2,1,0:T(8,128)}) fusion(f32[4,1024,256]{2,1,0:T(8,128)} %bitcast.20), kind=kLoop, calls=%fused_computation.26 | loop fusion | bytes 196608 | tf_op jit(solution)/shard_map/slice | solution.py:228
  12.3 1.6 %fusion.7 = (s32[2,1024,3]{2,1,0:T(8,128)}, s32[2,1024,3]{2,1,0:T(8,128)}) fusion(s32[2,1024,256]{2,1,0:T(8,128)S(1)} %copy-done.1), kind=kLoop, calls=%fused_computation.28 | loop fusion | bytes 98304 | tf_op jit(solution)/shard_map/slice | solution.py:228
  13.9 1.1 slice_bitcast_fusion.1
  15.0 2.2 %copy.8 = f32[4,1024,3]{1,0,2:T(4,128)S(1)} copy(f32[4,1024,3]{2,1,0:T(8,128)} %get-tuple-element.5) | data formatting | bytes 98304 | tf_op jit(solution)/shard_map/slice | solution.py:228
  17.2 1.6 %copy.19 = s32[2,1024,3]{1,0,2:T(2,128)S(1)} copy(s32[2,1024,3]{2,1,0:T(8,128)} %get-tuple-element.9) | data formatting | bytes 49152
  18.8 1.2 %copy.22 = f32[1,1024,3]{1,0,2:T(1,128)S(1)} copy(f32[1,1024,3]{2,1,0:T(8,128)} %get-tuple-element.13) | data formatting | bytes 24576 | tf_op jit(solution)/shard_map/broadcast_in_dim | solution.py:228
  20.7 1.6 %copy.21 = s32[2,1024,3]{1,0,2:T(2,128)S(1)} copy(s32[2,1024,3]{2,1,0:T(8,128)} %get-tuple-element.10) | data formatting | bytes 49152
  22.3 1.2 %copy.23 = f32[1,1024,3]{1,0,2:T(1,128)S(1)} copy(f32[1,1024,3]{2,1,0:T(8,128)} %get-tuple-element.14) | data formatting | bytes 24576 | tf_op jit(solution)/shard_map/broadcast_in_dim | solution.py:228
  23.6 14.1 %all_gather.3 = f32[7,3,1024]{2,1,0:T(4,128)S(1)} all-gather(f32[7,3,256]{2,1,0:T(4,128)S(1)} %pad_maximum_fusion.3), channel_id=1, replica_groups=mesh['lon'=4,'lat'=2,'mem'=4] {'lon'}, dimensions={2}, use_global_device_ids=true | all-gather | bytes 107520 | tf_op jit(solution)/shard_map/all_gather | solution.py:236
  37.7 0.9 rev.3
  39.5 3.4 %collective-permute-start.2 = (f32[7,3,1030]{2,0,1:T(8,128)S(1)}, f32[7,3,1030]{2,0,1:T(8,128)S(1)}, u32[]{:S(2)}, u32[]{:S(2)}) collective-permute-start(f32[7,3,1030]{2,0,1:T(8,128)S(1)} %bitcast.23), channel_id=1, source_target_pairs={{0,24},{8,0},{16,8},{24,16},{1,25},{9,1},{17,9},{25,17},{2,26},{10... | collective-permute-start | bytes 259568 | tf_op jit(solution)/shard_map/ppermute | solution.py:213
  43.4 2.0 %collective-permute-done.2 = f32[7,3,1030]{2,0,1:T(8,128)S(1)} collective-permute-done((f32[7,3,1030]{2,0,1:T(8,128)S(1)}, f32[7,3,1030]{2,0,1:T(8,128)S(1)}, u32[]{:S(2)}, u32[]{:S(2)}) %collective-permute-start.2) | collective-permute-done | bytes 86552 | tf_op jit(solution)/shard_map/ppermute | solution.py:213
  45.3 2.6 %copy.16 = f32[7,3,1030]{1,2,0:T(8,128)} copy(f32[7,3,1030]{2,0,1:T(8,128)S(1)} %collective-permute-done.2) | data formatting | bytes 173040 | tf_op jit(solution)/shard_map/ppermute | solution.py:213
  48.0 1.9 %collective-permute-done.3 = f32[7,3,1030]{2,0,1:T(8,128)S(1)} collective-permute-done((f32[7,3,1030]{2,0,1:T(8,128)S(1)}, f32[7,3,1030]{2,0,1:T(8,128)S(1)}, u32[]{:S(2)}, u32[]{:S(2)}) %collective-permute-start.3) | collective-permute-done | bytes 86552 | tf_op jit(solution)/shard_map/ppermute | solution.py:213
  49.9 2.6 %copy.17 = f32[7,3,1030]{1,2,0:T(8,128)} copy(f32[7,3,1030]{2,0,1:T(8,128)S(1)} %collective-permute-done.3) | data formatting | bytes 173040 | tf_op jit(solution)/shard_map/ppermute | solution.py:213
  52.4 4.2 %maximum_bitcast_fusion = f32[7,1030,128]{2,1,0:T(8,128)S(1)} fusion(f32[7,3,1030]{1,2,0:T(8,128)} %copy.17, f32[7,3,1030]{1,2,0:T(8,128)} %copy.16, f32[128]{0:T(128)S(1)} %pad.18.clone), kind=kLoop, calls=%fused_computation | loop fusion | flops 1845760 | bytes 3865072 | tf_op jit(solution)/shard_map/transpose | solution.py:253
  56.6 1.7 %pad_slice_fusion.1.side_f = f32[5,1040,128]{2,1,0:T(8,128)} fusion(f32[7,1030,128]{2,1,0:T(8,128)S(1)} %maximum_bitcast_fusion), kind=kLoop, calls=%fused_computation.2 | loop fusion | bytes 6353920 | tf_op jit(solution)/shard_map/slice | solution.py:298
  58.5 59.1 %shard_map.55 = f32[2,1024,256]{2,1,0:T(8,128)} custom-call(f32[4,1024,256]{2,1,0:T(8,128)} %bitcast.21, f32[4,1024,256]{2,1,0:T(8,128)} %bitcast.22, f32[1024,256]{1,0:T(8,128)S(1)} %copy-done, s32[2,1024,256]{2,1,0:T(8,128)} %sea.1, f32[5,1040,128]{2,1,0:T(8,128)} %pad_slice_fusion.1.side_f, s32[2,1040,128]{2,1,0:T(8,128)S(1)} %fusion.side_i, ...), custom_call_target="tpu_custom_call" | custom-call | flops 41943040 | bytes 16777216 | tf_op jit(solution)/shard_map/pallas_call | solution.py:268
  117.6 3.0 %copy.25 = f32[2,1024,256]{2,1,0:T(8,128)} copy(f32[2,1024,256]{2,1,0:T(8,128)} %shard_map.55) | data formatting | bytes 4194304
  (34 shorter events, 2.2 us)
Async XLA Ops:
  2.3 36.5 %collective-permute-start.1 = (f32[7,3,256]{2,1,0:T(4,128)S(1)}, f32[7,3,256]{2,1,0:T(4,128)S(1)}, u32[]{:S(2)}, u32[]{:S(2)}) collective-permute-start(f32[7,3,256]{2,1,0:T(4,128)S(1)} %pad_maximum_fusion.4), channel_id=1, source_target_pairs={{0,4},{4,0},{1,5},{5,1},{2,6},{6,2},{3,7},{7,3},{8,12},{12,8},{9,1... | collective-permute-start | bytes 64520 | tf_op jit(solution)/shard_map/ppermute | solution.py:213
  5.3 33.7 %collective-permute-start = (f32[7,3,256]{2,1,0:T(4,128)S(1)}, f32[7,3,256]{2,1,0:T(4,128)S(1)}, u32[]{:S(2)}, u32[]{:S(2)}) collective-permute-start(f32[7,3,256]{2,1,0:T(4,128)S(1)} %pad_maximum_fusion.3), channel_id=1, source_target_pairs={{0,4},{4,0},{1,5},{5,1},{2,6},{6,2},{3,7},{7,3},{8,12},{12,8},{9,1... | collective-permute-start | bytes 64520 | tf_op jit(solution)/shard_map/ppermute | solution.py:213
  7.2 5.0 %copy-start.1 = (s32[2,1024,256]{2,1,0:T(8,128)S(1)}, s32[2,1024,256]{2,1,0:T(8,128)}, u32[]{:S(2)}) copy-start(s32[2,1024,256]{2,1,0:T(8,128)} %sea.1) | copy-start | bytes 6291460
  12.3 1.6 %copy-start = (f32[1024,256]{1,0:T(8,128)S(1)}, f32[1024,256]{1,0:T(8,128)}, u32[]{:S(2)}) copy-start(f32[1024,256]{1,0:T(8,128)} %kappa.1) | copy-start | bytes 3145732
  13.9 6.2 %copy-start.2 = (f32[4,1024,3]{2,1,0:T(8,128)S(1)}, f32[4,1024,3]{2,1,0:T(8,128)}, u32[]{:S(2)}) copy-start(f32[4,1024,3]{2,1,0:T(8,128)} %get-tuple-element.6) | copy-start | bytes 147460
  39.5 5.9 %collective-permute-start.2 = (f32[7,3,1030]{2,0,1:T(8,128)S(1)}, f32[7,3,1030]{2,0,1:T(8,128)S(1)}, u32[]{:S(2)}, u32[]{:S(2)}) collective-permute-start(f32[7,3,1030]{2,0,1:T(8,128)S(1)} %bitcast.23), channel_id=1, source_target_pairs={{0,24},{8,0},{16,8},{24,16},{1,25},{9,1},{17,9},{25,17},{2,26},{10... | collective-permute-start | bytes 259568 | tf_op jit(solution)/shard_map/ppermute | solution.py:213
  43.3 6.6 %collective-permute-start.3 = (f32[7,3,1030]{2,0,1:T(8,128)S(1)}, f32[7,3,1030]{2,0,1:T(8,128)S(1)}, u32[]{:S(2)}, u32[]{:S(2)}) collective-permute-start(f32[7,3,1030]{2,0,1:T(8,128)S(1)} %bitcast.24), channel_id=1, source_target_pairs={{0,8},{8,16},{16,24},{24,0},{1,9},{9,17},{17,25},{25,1},{2,10},{10... | collective-permute-start | bytes 259568 | tf_op jit(solution)/shard_map/ppermute | solution.py:213
where the time goes:
time: 121 us
  Pallas kernels  59.1 us (49%)
  local copies, waits for them, and re-layouts  30.8 us (25%)
  blocking collectives  14.1 us (12%)
  starting transfers between devices  6.54 us (5%)
  other arithmetic  5.35 us (4%)
  waiting for transfers between devices  3.9 us (3%)
    pallas_call x1, Pallas kernels, per_device(): pl.pallas_call(kernel, out_shape=jax.ShapeDtypeStruct((levels, rows, cols...  59.1 us
    all_gather x1, blocking collectives, per_device(): gathered = lax.all_gather(north_edge, 'lon', axis=2, tiled=True)  14.1 us
    slice x4, local copies, waits for them, and re-layouts, cut(): flat[:, r, c]  8.65 us
    ppermute x4, starting transfers between devices, shifted(): lax.ppermute(block, axis, [(i, (i + by) % count) for i in range(count)])  6.54 us
    unnamed x9, local copies, waits for them, and re-layouts  6.19 us
    ppermute x2, local copies, waits for them, and re-layouts, shifted(): lax.ppermute(block, axis, [(i, (i + by) % count) for i in range(count)])  5.19 us
    broadcast_in_dim x4, local copies, waits for them, and re-layouts, cut(): diffusivity[None, r, c]  4.28 us
    transpose x1, other arithmetic, per_device(): jnp.swapaxes(jnp.concatenate([from_east, middle, from_west], axis=1), 1, 2)  4.19 us
  transfers between devices with their start and end apart: 4, of which 2 were waited for; matrix products, arithmetic and copies ran while one was open for 18% of the time, Pallas kernels for 0%

commit v1 on v0

v1 whole, which is shorter than its diff:
```python
import jax
import jax.numpy as jnp
from jax import lax
from jax.experimental import pallas as pl
from jax.experimental.pallas import tpu as pltpu
from jax.sharding import PartitionSpec as P

PASSES = 3
CHUNK = 128
STEP = 4
PAD = 4
LEAD = 10
TAIL = 16
MESH = pl.DeviceIdType.MESH


def kernel(
    control, perturb, kappa, sea, pivot, out,
    field, once, again, weight, kap, mask, sea_int, g_east, g_north, state,
    pack, pack_in, top, top_in,
    part, part_in, pair, pair_in, total,
    in_sem, side_send, side_recv, rim_send, rim_recv, top_send, top_recv,
    a_send, a_recv, b_send, b_recv, c_send, c_recv, o_sem,
):
    fields, rows, cols = control.shape
    levels = fields // 2
    wide = cols + 128
    blocks = rows // 8
    chunks = rows // CHUNK
    per_chunk = CHUNK // 8
    count = lax.axis_size("lon")
    lon = lax.axis_index("lon")
    lat = lax.axis_index("lat")
    mem = lax.axis_index("mem")
    core = lax.rem(mem, 2)
    twin = {"mem": mem + 1 - 2 * core}
    across = {"mem": lax.rem(mem + 2, 4)}
    facing = {"lat": 1 - lat}
    lon_peer = [None] + [{"lon": lax.rem(lon + d, count)} for d in range(1, count)]
    east_peer = lon_peer[1]
    west_peer = lon_peer[count - 1]
    bottom_band = lat == 0
    top_band = lat == 1

    body_rows = pl.ds(PAD * 8, rows)
    loads = [
        pltpu.make_async_copy(control, field.at[:, body_rows, 0:cols], in_sem.at[0]),
        pltpu.make_async_copy(kappa, kap.at[body_rows, 0:cols], in_sem.at[1]),
        pltpu.make_async_copy(sea, sea_int, in_sem.at[2]),
        pltpu.make_async_copy(perturb, weight, in_sem.at[3]),
    ]
    for copy in loads:
        copy.start()

    barrier = pltpu.get_barrier_semaphore()
    peers = lon_peer[1:] + [facing, twin, across]
    for peer in peers:
        pl.semaphore_signal(barrier, inc=1, device_id=peer, device_id_type=MESH)
    for copy in loads[:3]:
        copy.wait()

    row_id = lax.broadcasted_iota(jnp.int32, (8, wide), 0)
    first = row_id == 0
    last = row_id == 7
    lane = lax.broadcasted_iota(jnp.int32, (8, 128), 1)

    def block(idx):
        return pl.ds(pl.multiple_of((idx + PAD) * 8, 8), 8)

    def plain(idx):
        return pl.ds(pl.multiple_of(idx * 8, 8), 8)

    def source(item, idx, c):
        if item < fields:
            return field[item, block(idx), c]
        if item == fields:
            return kap[block(idx), c]
        return mask[item - fields - 1, block(idx), c]

    def store(item, idx, c, value):
        if item < fields:
            field[item, block(idx), c] = value
        elif item == fields:
            kap[block(idx), c] = value
        else:
            mask[item - fields - 1, block(idx), c] = value

    items = fields + 1 + levels
    groups = 4
    quarter = blocks // groups
    slot_of = lambda item, g: g * (128 // groups) + item * PASSES
    left = slice(0, 128)
    right = slice(cols - 128, cols)
    extra = slice(cols, wide)

    @pl.loop(0, quarter)
    def _(b):
        west = jnp.zeros((8, 128), jnp.float32)
        east = jnp.zeros((8, 128), jnp.float32)
        for g in range(groups):
            idx = g * quarter + b
            for lev in range(levels):
                mask[lev, block(idx), 0:cols] = sea_int[lev, plain(idx)].astype(jnp.float32)
            for item in range(items):
                slot = slot_of(item, g)
                here = jnp.logical_and(lane >= slot, lane < slot + PASSES)
                if item <= fields:
                    lo = source(item, idx, left)
                    hi = source(item, idx, right)
                else:
                    lo = sea_int[item - fields - 1, plain(idx), left].astype(jnp.float32)
                    hi = sea_int[item - fields - 1, plain(idx), right].astype(jnp.float32)
                if slot:
                    lo = pltpu.roll(lo, slot, 1)
                west = jnp.where(here, lo, west)
                east = jnp.where(here, pltpu.roll(hi, slot + PASSES, 1), east)
        pack[0, plain(b)] = west
        pack[1, plain(b)] = east

    for item in range(items):
        top[item] = source(item, blocks - 1, slice(0, cols))

    pl.semaphore_wait(barrier, len(peers))

    def side_copy(way, peer):
        return pltpu.make_async_remote_copy(
            src_ref=pack.at[way], dst_ref=pack_in.at[way], send_sem=side_send.at[way],
            recv_sem=side_recv.at[way], device_id=peer, device_id_type=MESH,
        )

    sides = [side_copy(0, west_peer), side_copy(1, east_peer)]
    for copy in sides:
        copy.start()
    gathers = [
        pltpu.make_async_remote_copy(
            src_ref=top, dst_ref=top_in.at[d - 1], send_sem=top_send.at[d - 1],
            recv_sem=top_recv.at[d - 1], device_id=lon_peer[d], device_id_type=MESH,
        )
        for d in range(1, count)
    ]
    for copy in gathers:
        copy.start()
    for copy in sides:
        copy.wait_recv()

    @pl.loop(0, quarter)
    def _(b):
        from_east = pack_in[0, plain(b)]
        from_west = pack_in[1, plain(b)]
        for g in range(groups):
            for item in range(items):
                slot = slot_of(item, g)
                near = pltpu.roll(from_east, 128 - slot, 1) if slot else from_east
                far = pltpu.roll(from_west, 128 - slot - PASSES, 1)
                store(item, g * quarter + b, extra, jnp.where(lane < 64, near, far))

    rim_from = block((blocks - 1) * (1 - lat))
    rim_to = block(lat * (blocks + 1) - 1)
    rims = [
        pltpu.make_async_remote_copy(
            src_ref=src, dst_ref=dst, send_sem=rim_send.at[i], recv_sem=rim_recv.at[i],
            device_id=facing, device_id_type=MESH,
        )
        for i, (src, dst) in enumerate((
            (field.at[:, rim_from], field.at[:, rim_to]),
            (kap.at[rim_from], kap.at[rim_to]),
            (mask.at[:, rim_from], mask.at[:, rim_to]),
        ))
    ]
    for copy in rims:
        copy.start()

    @pl.when(bottom_band)
    def _():
        for item in range(items):
            store(item, -1, slice(0, wide), jnp.zeros((8, wide), jnp.float32))

    loads[3].wait()
    for copy in rims:
        copy.wait_recv()

    def fold():
        lanes = lax.broadcasted_iota(jnp.int32, (cols, wide), 1)
        offset = lax.broadcasted_iota(jnp.int32, (cols, wide), 0)
        span = count * cols
        column = lon * cols + jnp.where(lanes < cols + 64, lanes, lanes - wide)
        aim = pivot[0] - column - offset
        acc = jnp.zeros((items * 8, wide), jnp.float32)
        for d in range(count):
            origin = lax.rem(lon + count - d, count) * cols
            gap = aim - origin
            hit = gap == 0
            for turn in (span, -span, -2 * span):
                hit = jnp.logical_or(hit, gap == turn)
            held = top[...] if d == 0 else top_in[d - 1]
            acc = acc + lax.dot_general(
                held.reshape(items * 8, cols), jnp.where(hit, 1.0, 0.0),
                (((1,), (0,)), ((), ())), precision=lax.Precision.HIGHEST,
                preferred_element_type=jnp.float32,
            )
        for item in range(items):
            rows8 = acc[item * 8 : item * 8 + 8]
            ghost = jnp.where(
                first, pltpu.roll(rows8, 1, 0),
                jnp.where(row_id == 1, pltpu.roll(rows8, 3, 0), pltpu.roll(rows8, 5, 0)),
            )
            store(item, blocks, slice(0, wide), ghost)

    def up(cur, nxt):
        return pltpu.roll(jnp.where(first, nxt, cur), 7, 0)

    def sweep(origin, gauges, before):
        results = []
        for i in range(STEP):
            cur = origin[i]
            ge, gn = gauges[i]
            north = gn * (up(cur, origin[i + 1]) - cur)
            south = pltpu.roll(jnp.where(last, before, north), 1, 0)
            east = ge * (pltpu.roll(cur, wide - 1, 1) - cur)
            west = pltpu.roll(east, 1, 1)
            results.append(cur + ((east - west) + (north - south)))
            before = north
        return results, before

    def advance(level, a, depth, emit=None):
        held = [[state[level, m, p] for p in range(depth)] for m in range(2)]
        for p in range(depth - 1, -1, -1):
            at = a - 5 * p
            origin_ref = (field, once, again)[p]
            gauges = [
                (g_east[level, block(at + i)], g_north[level, block(at + i)]) for i in range(STEP)
            ]
            finals = []
            for m in range(2):
                n = levels * m + level
                origin = [origin_ref[n, block(at + i)] for i in range(STEP + 1)]
                results, held[m][p] = sweep(origin, gauges, held[m][p])
                if p < 2:
                    for i in range(STEP):
                        (once, again)[p][n, block(at + i)] = results[i]
                finals.append(results)
            if p == 2 and emit is not None:
                emit(finals)
        for m in range(2):
            for p in range(depth):
                state[level, m, p] = held[m][p]
        at = a + STEP
        ks = [kap[block(at + i)] for i in range(STEP + 1)]
        ss = [mask[level, block(at + i)] for i in range(STEP + 1)]
        for i in range(STEP):
            half = 0.5 * ss[i]
            g_north[level, block(at + i)] = (ks[i] + up(ks[i], ks[i + 1])) * (
                half * up(ss[i], ss[i + 1])
            )
            g_east[level, block(at + i)] = (ks[i] + pltpu.roll(ks[i], wide - 1, 1)) * (
                half * pltpu.roll(ss[i], wide - 1, 1)
            )

    @pl.loop(0, levels)
    def _(level):
        for depth in range(4):
            advance(level, LEAD - TAIL + STEP * depth, depth)

    def diffuse_chunk(k, level, into):
        @pl.loop(0, per_chunk // STEP)
        def _(j):
            o = k * per_chunk + j * STEP

            def emit(finals):
                for i in range(STEP):
                    acc = weight[level, plain(o + i)] * finals[0][i][:, 0:cols]
                    acc = acc + weight[levels + level, plain(o + i)] * finals[1][i][:, 0:cols]
                    into[k, plain(j * STEP + i)] = acc

            advance(level, o + LEAD, 3, emit)

    def send_part(k):
        return pltpu.make_async_remote_copy(
            src_ref=part.at[k], dst_ref=part_in.at[k], send_sem=a_send.at[k],
            recv_sem=a_recv.at[k], device_id=twin, device_id_type=MESH,
        )

    def send_pair(k):
        return pltpu.make_async_remote_copy(
            src_ref=pair.at[k], dst_ref=pair_in.at[k], send_sem=b_send.at[k],
            recv_sem=b_recv.at[k], device_id=across, device_id_type=MESH,
        )

    def chunk_rows(k):
        return pl.ds(pl.multiple_of(k * CHUNK, CHUNK), CHUNK)

    def send_total(k):
        return pltpu.make_async_remote_copy(
            src_ref=total.at[k], dst_ref=out.at[core, chunk_rows(k)], send_sem=c_send.at[k],
            recv_sem=c_recv.at[k], device_id=twin, device_id_type=MESH,
        )

    def store_total(k):
        return pltpu.make_async_copy(total.at[k], out.at[core, chunk_rows(k)], o_sem.at[k])

    @pl.loop(0, chunks)
    def _(k):
        @pl.when(k == chunks - 2)
        def _():
            for copy in gathers:
                copy.wait_recv()

            @pl.when(top_band)
            def _():
                fold()

        diffuse_chunk(k, 1 - core, part)
        send_part(k).start()
        diffuse_chunk(k, core, pair)
        send_part(k).wait_recv()

        @pl.loop(0, per_chunk)
        def _(j):
            pair[k, plain(j)] = pair[k, plain(j)] + part_in[k, plain(j)]

        send_pair(k).start()

    @pl.loop(0, chunks)
    def _(k):
        send_pair(k).wait_recv()

        @pl.loop(0, per_chunk)
        def _(j):
            sea_here = mask[core, block(k * per_chunk + j), 0:cols]
            total[k, plain(j)] = (pair[k, plain(j)] + pair_in[k, plain(j)]) * sea_here

        send_total(k).start()
        store_total(k).start()

    @pl.loop(0, chunks)
    def _(k):
        send_part(k).wait_send()
        send_pair(k).wait_send()
        send_total(k).wait()
        store_total(k).wait()

    for copy in sides + gathers + rims:
        copy.wait_send()


def per_device(perturb, control, diffusivity, sea_mask, fold_partner):
    members, levels, rows, cols = control.shape
    fields = members * levels
    chunks = rows // CHUNK
    wide = cols + 128
    tall = rows + 8 * (PAD + TAIL)
    items = fields + 1 + levels
    count = lax.axis_size("lon")
    f32 = jnp.float32
    any_spec = pl.BlockSpec(memory_space=pl.ANY)
    chunk_buf = pltpu.VMEM((chunks, CHUNK, cols), f32)
    full = pltpu.VMEM((fields, tall, wide), f32)
    by_level = pltpu.VMEM((levels, tall, wide), f32)
    packed = pltpu.VMEM((2, rows // 4, 128), f32)
    dma = pltpu.SemaphoreType.DMA
    return pl.pallas_call(
        kernel,
        out_shape=jax.ShapeDtypeStruct((levels, rows, cols), f32),
        in_specs=[any_spec] * 4 + [pl.BlockSpec(memory_space=pltpu.SMEM)],
        out_specs=any_spec,
        scratch_shapes=[
            full, full, full,
            pltpu.VMEM((fields, rows, cols), f32),
            pltpu.VMEM((tall, wide), f32),
            by_level,
            pltpu.VMEM((levels, rows, cols), jnp.int32),
            by_level, by_level,
            pltpu.VMEM((levels, members, PASSES, 8, wide), f32),
            packed, packed,
            pltpu.VMEM((items, 8, cols), f32),
            pltpu.VMEM((count - 1, items, 8, cols), f32),
            chunk_buf, chunk_buf, chunk_buf, chunk_buf, chunk_buf,
            dma((4,)), dma((2,)), dma((2,)), dma((3,)), dma((3,)),
            dma((count - 1,)), dma((count - 1,)),
            dma((chunks,)), dma((chunks,)), dma((chunks,)), dma((chunks,)),
            dma((chunks,)), dma((chunks,)), dma((chunks,)),
        ],
        compiler_params=pltpu.CompilerParams(
            collective_id=0, has_side_effects=True, vmem_limit_bytes=60 * 1024 * 1024
        ),
        cost_estimate=pl.CostEstimate(
            flops=40 * fields * rows * cols, bytes_accessed=16 * fields * rows * cols, transcendentals=0
        ),
    )(
        control.reshape(fields, rows, cols),
        perturb.reshape(fields, rows, cols),
        diffusivity,
        sea_mask,
        fold_partner[:1],
    )


def solution(mesh):
    return jax.shard_map(
        per_device,
        mesh=mesh,
        in_specs=(
            P("mem", None, "lat", "lon"),
            P("mem", None, "lat", "lon"),
            P("lat", "lon"),
            P(None, "lat", "lon"),
            P(),
        ),
        out_specs=P(None, "lat", "lon"),
        check_vma=False,
    )
```

time: 121 us -> 83.2 us (0.69)
  local copies, waits for them, and re-layouts: 30.8 us -> 4.24 us
  Pallas kernels: 59.1 us -> 78.8 us
  blocking collectives: 14.1 us -> 0 us
  starting transfers between devices: 6.54 us -> 0 us
  other arithmetic: 5.35 us -> 0 us
  waiting for transfers between devices: 3.9 us -> 0 us
    pallas_call x1, Pallas kernels: 59.1 us -> 78.8 us  [per_device(): pl.pallas_call(kernel, out_shape=jax.ShapeDtypeStruct((levels, rows, cols...]
    all_gather x1 -> x0, blocking collectives: 14.1 us -> none  [per_device(): gathered = lax.all_gather(north_edge, 'lon', axis=2, tiled=True)]
    slice x13 -> x1, local copies, waits for them, and re-layouts: 13.9 us -> 1.2 us  [per_device(): fold_partner[:1]]
    ppermute x4 -> x0, starting transfers between devices: 6.54 us -> none  [shifted(): lax.ppermute(block, axis, [(i, (i + by) % count) for i in range(count)])]
    ppermute x2 -> x0, local copies, waits for them, and re-layouts: 5.19 us -> none  [shifted(): lax.ppermute(block, axis, [(i, (i + by) % count) for i in range(count)])]
    broadcast_in_dim x5 -> x0, local copies, waits for them, and re-layouts: 4.29 us -> none  [the longest x4 4.28 us: cut(): diffusivity[None, r, c]]
    transpose x1 -> x0, other arithmetic: 4.19 us -> none  [per_device(): jnp.swapaxes(jnp.concatenate([from_east, middle, from_west], axis=1), 1, 2)]
    ppermute x4 -> x0, waiting for transfers between devices: 3.9 us -> none  [shifted(): lax.ppermute(block, axis, [(i, (i + by) % count) for i in range(count)])]
  transfers between devices with their start and end apart: 4 -> 0, of which waited for: 2 -> 0; matrix products, arithmetic and copies ran while one was open for 18% -> 0% of each run, Pallas kernels for 0% -> 0%
where the time goes in v1:
time: 83.2 us; the launch traced here: 83 us
  Pallas kernels  78.8 us (95%)
  local copies, waits for them, and re-layouts  4.24 us (5%)
    pallas_call x1, Pallas kernels, per_device(): pl.pallas_call(kernel, out_shape=jax.ShapeDtypeStruct((levels, rows, cols...  78.8 us
    unnamed x1, local copies, waits for them, and re-layouts  3.05 us

profile of v1, /device:TPU:0, one launch (start us, length us, event | category | flops | bytes accessed | tf_op | source)
XLA Modules:
  0.0 83.0 jit_solution(3087965039979290629)
XLA Ops:
  0.0 1.2 %slice.3.pivot = s32[1]{0:T(128)} slice(s32[1024]{0:T(1024)} %param.9), slice={[0:1]} | slice | bytes 8 | tf_op jit(solution)/shard_map/slice | solution.py:394
  1.2 78.8 %shard_map.55 = f32[2,1024,256]{2,1,0:T(8,128)} custom-call(f32[4,1024,256]{2,1,0:T(8,128)} %bitcast.2, f32[4,1024,256]{2,1,0:T(8,128)} %bitcast.3, f32[1024,256]{1,0:T(8,128)} %kappa.1, s32[2,1024,256]{2,1,0:T(8,128)} %sea.1, s32[1]{0:T(128)} %slice.3.pivot), custom_call_target="tpu_custom_call" | custom-call | flops 41943040 | bytes 16777216 | tf_op jit(solution)/shard_map/pallas_call | solution.py:361
  80.0 3.0 %copy.7 = f32[2,1024,256]{2,1,0:T(8,128)} copy(f32[2,1024,256]{2,1,0:T(8,128)} %shard_map.55) | data formatting | bytes 4194304

commit v2 on v1

--- a/solution.py
+++ b/solution.py
@@ -11,12 +11,13 @@
 PAD = 4
 LEAD = 10
 TAIL = 16
+LANES = 128
 MESH = pl.DeviceIdType.MESH
 
 
 def kernel(
     control, perturb, kappa, sea, pivot, out,
-    field, once, again, weight, kap, mask, sea_int, g_east, g_north, state,
+    field, once, again, weight, kap, mask, sea_int, g_mid, g_east, g_west, g_north,
     pack, pack_in, top, top_in,
     part, part_in, pair, pair_in, total,
     in_sem, side_send, side_recv, rim_send, rim_recv, top_send, top_recv,
@@ -24,7 +25,8 @@
 ):
     fields, rows, cols = control.shape
     levels = fields // 2
-    wide = cols + 128
+    tiles = cols // LANES
+    wide = cols + LANES
     blocks = rows // 8
     chunks = rows // CHUNK
     per_chunk = CHUNK // 8
@@ -44,11 +46,15 @@
 
     body_rows = pl.ds(PAD * 8, rows)
     loads = [
-        pltpu.make_async_copy(control, field.at[:, body_rows, 0:cols], in_sem.at[0]),
-        pltpu.make_async_copy(kappa, kap.at[body_rows, 0:cols], in_sem.at[1]),
-        pltpu.make_async_copy(sea, sea_int, in_sem.at[2]),
-        pltpu.make_async_copy(perturb, weight, in_sem.at[3]),
+        pltpu.make_async_copy(sea, sea_int, in_sem.at[0]),
+        pltpu.make_async_copy(perturb, weight, in_sem.at[1]),
     ]
+    for t in range(tiles):
+        span = slice(t * LANES, (t + 1) * LANES)
+        loads += [
+            pltpu.make_async_copy(control.at[:, :, span], field.at[:, t, body_rows], in_sem.at[2 + 2 * t]),
+            pltpu.make_async_copy(kappa.at[:, span], kap.at[t, body_rows], in_sem.at[3 + 2 * t]),
+        ]
     for copy in loads:
         copy.start()
 
@@ -56,42 +62,40 @@
     peers = lon_peer[1:] + [facing, twin, across]
     for peer in peers:
         pl.semaphore_signal(barrier, inc=1, device_id=peer, device_id_type=MESH)
-    for copy in loads[:3]:
+    for copy in loads[:1] + loads[2:]:
         copy.wait()
 
     row_id = lax.broadcasted_iota(jnp.int32, (8, wide), 0)
     first = row_id == 0
-    last = row_id == 7
     lane = lax.broadcasted_iota(jnp.int32, (8, 128), 1)
 
-    def block(idx):
-        return pl.ds(pl.multiple_of((idx + PAD) * 8, 8), 8)
+    def block(idx, by=0):
+        return pl.ds(pl.multiple_of((idx + PAD) * 8, 8) + by, 8)
 
     def plain(idx):
         return pl.ds(pl.multiple_of(idx * 8, 8), 8)
 
-    def source(item, idx, c):
+    def source(item, idx, t):
         if item < fields:
-            return field[item, block(idx), c]
+            return field[item, t, block(idx)]
         if item == fields:
-            return kap[block(idx), c]
-        return mask[item - fields - 1, block(idx), c]
-
-    def store(item, idx, c, value):
+            return kap[t, block(idx)]
+        return mask[item - fields - 1, t, block(idx)]
+
+    def store(item, idx, t, value):
         if item < fields:
-            field[item, block(idx), c] = value
+            field[item, t, block(idx)] = value
         elif item == fields:
-            kap[block(idx), c] = value
+            kap[t, block(idx)] = value
         else:
-            mask[item - fields - 1, block(idx), c] = value
+            mask[item - fields - 1, t, block(idx)] = value
 
     items = fields + 1 + levels
     groups = 4
     quarter = blocks // groups
     slot_of = lambda item, g: g * (128 // groups) + item * PASSES
-    left = slice(0, 128)
-    right = slice(cols - 128, cols)
-    extra = slice(cols, wide)
+    left = 0
+    right = tiles - 1
 
     @pl.loop(0, quarter)
     def _(b):
@@ -100,7 +104,9 @@
         for g in range(groups):
             idx = g * quarter + b
             for lev in range(levels):
-                mask[lev, block(idx), 0:cols] = sea_int[lev, plain(idx)].astype(jnp.float32)
+                for t in range(tiles):
+                    span = slice(t * LANES, (t + 1) * LANES)
+                    mask[lev, t, block(idx)] = sea_int[lev, plain(idx), span].astype(jnp.float32)
             for item in range(items):
                 slot = slot_of(item, g)
                 here = jnp.logical_and(lane >= slot, lane < slot + PASSES)
@@ -108,8 +114,8 @@
                     lo = source(item, idx, left)
                     hi = source(item, idx, right)
                 else:
-                    lo = sea_int[item - fields - 1, plain(idx), left].astype(jnp.float32)
-                    hi = sea_int[item - fields - 1, plain(idx), right].astype(jnp.float32)
+                    lo = sea_int[item - fields - 1, plain(idx), 0:LANES].astype(jnp.float32)
+                    hi = sea_int[item - fields - 1, plain(idx), cols - LANES : cols].astype(jnp.float32)
                 if slot:
                     lo = pltpu.roll(lo, slot, 1)
                 west = jnp.where(here, lo, west)
@@ -118,7 +124,8 @@
         pack[1, plain(b)] = east
 
     for item in range(items):
-        top[item] = source(item, blocks - 1, slice(0, cols))
+        for t in range(tiles):
+            top[item, :, t * LANES : (t + 1) * LANES] = source(item, blocks - 1, t)
 
     pl.semaphore_wait(barrier, len(peers))
 
@@ -152,7 +159,7 @@
                 slot = slot_of(item, g)
                 near = pltpu.roll(from_east, 128 - slot, 1) if slot else from_east
                 far = pltpu.roll(from_west, 128 - slot - PASSES, 1)
-                store(item, g * quarter + b, extra, jnp.where(lane < 64, near, far))
+                store(item, g * quarter + b, tiles, jnp.where(lane < 64, near, far))
 
     rim_from = block((blocks - 1) * (1 - lat))
     rim_to = block(lat * (blocks + 1) - 1)
@@ -162,9 +169,9 @@
             device_id=facing, device_id_type=MESH,
         )
         for i, (src, dst) in enumerate((
-            (field.at[:, rim_from], field.at[:, rim_to]),
-            (kap.at[rim_from], kap.at[rim_to]),
-            (mask.at[:, rim_from], mask.at[:, rim_to]),
+            (field.at[:, :, rim_from], field.at[:, :, rim_to]),
+            (kap.at[:, rim_from], kap.at[:, rim_to]),
+            (mask.at[:, :, rim_from], mask.at[:, :, rim_to]),
         ))
     ]
     for copy in rims:
@@ -173,9 +180,10 @@
     @pl.when(bottom_band)
     def _():
         for item in range(items):
-            store(item, -1, slice(0, wide), jnp.zeros((8, wide), jnp.float32))
-
-    loads[3].wait()
+            for t in range(tiles + 1):
+                store(item, -1, t, jnp.zeros((8, LANES), jnp.float32))
+
+    loads[1].wait()
     for copy in rims:
         copy.wait_recv()
 
@@ -204,73 +212,89 @@
                 first, pltpu.roll(rows8, 1, 0),
                 jnp.where(row_id == 1, pltpu.roll(rows8, 3, 0), pltpu.roll(rows8, 5, 0)),
             )
-            store(item, blocks, slice(0, wide), ghost)
-
-    def up(cur, nxt):
-        return pltpu.roll(jnp.where(first, nxt, cur), 7, 0)
-
-    def sweep(origin, gauges, before):
-        results = []
+            for t in range(tiles + 1):
+                store(item, blocks, t, ghost[:, t * LANES : (t + 1) * LANES])
+
+    lane_first = lane == 0
+    lane_last = lane == LANES - 1
+
+    def eastward(values):
+        turned = [pltpu.roll(v, LANES - 1, 1) for v in values]
+        return [
+            jnp.where(lane_last, turned[(t + 1) % len(values)], turned[t])
+            for t in range(len(values))
+        ]
+
+    def westward(values):
+        turned = [pltpu.roll(v, 1, 1) for v in values]
+        return [jnp.where(lane_first, turned[t - 1], turned[t]) for t in range(len(values))]
+
+    every = range(tiles + 1)
+
+    def advance(level, a, depth, emit=None):
+        for p in range(depth - 1, -1, -1):
+            origin = (field, once, again)[p]
+            for i in range(STEP):
+                at = a - 5 * p + i
+                used = range(tiles) if p == 2 else every
+                gains = [
+                    (
+                        g_mid[level, t, block(at)], g_east[level, t, block(at)],
+                        g_west[level, t, block(at)], g_north[level, t, block(at)],
+                        g_north[level, t, block(at, -1)],
+                    )
+                    for t in used
+                ]
+                finals = []
+                for m in range(2):
+                    n = levels * m + level
+                    cur = [origin[n, t, block(at)] for t in every]
+                    east = eastward(cur)
+                    west = westward(cur)
+                    for t in used:
+                        gm, ge, gw, gn, gs = gains[t]
+                        value = (gm * cur[t] + (ge * east[t] + gw * west[t])) + (
+                            gn * origin[n, t, block(at, 1)] + gs * origin[n, t, block(at, -1)]
+                        )
+                        if p < 2:
+                            (once, again)[p][n, t, block(at)] = value
+                        else:
+                            finals.append(value)
+                if p == 2:
+                    emit(i, finals)
         for i in range(STEP):
-            cur = origin[i]
-            ge, gn = gauges[i]
-            north = gn * (up(cur, origin[i + 1]) - cur)
-            south = pltpu.roll(jnp.where(last, before, north), 1, 0)
-            east = ge * (pltpu.roll(cur, wide - 1, 1) - cur)
-            west = pltpu.roll(east, 1, 1)
-            results.append(cur + ((east - west) + (north - south)))
-            before = north
-        return results, before
-
-    def advance(level, a, depth, emit=None):
-        held = [[state[level, m, p] for p in range(depth)] for m in range(2)]
-        for p in range(depth - 1, -1, -1):
-            at = a - 5 * p
-            origin_ref = (field, once, again)[p]
-            gauges = [
-                (g_east[level, block(at + i)], g_north[level, block(at + i)]) for i in range(STEP)
-            ]
-            finals = []
-            for m in range(2):
-                n = levels * m + level
-                origin = [origin_ref[n, block(at + i)] for i in range(STEP + 1)]
-                results, held[m][p] = sweep(origin, gauges, held[m][p])
-                if p < 2:
-                    for i in range(STEP):
-                        (once, again)[p][n, block(at + i)] = results[i]
-                finals.append(results)
-            if p == 2 and emit is not None:
-                emit(finals)
-        for m in range(2):
-            for p in range(depth):
-                state[level, m, p] = held[m][p]
-        at = a + STEP
-        ks = [kap[block(at + i)] for i in range(STEP + 1)]
-        ss = [mask[level, block(at + i)] for i in range(STEP + 1)]
-        for i in range(STEP):
-            half = 0.5 * ss[i]
-            g_north[level, block(at + i)] = (ks[i] + up(ks[i], ks[i + 1])) * (
-                half * up(ss[i], ss[i + 1])
-            )
-            g_east[level, block(at + i)] = (ks[i] + pltpu.roll(ks[i], wide - 1, 1)) * (
-                half * pltpu.roll(ss[i], wide - 1, 1)
-            )
+            at = a + STEP + i
+            ks = [kap[t, block(at)] for t in every]
+            ss = [mask[level, t, block(at)] for t in every]
+            k_east, s_east = eastward(ks), eastward(ss)
+            k_west, s_west = westward(ks), westward(ss)
+            for t in every:
+                half = 0.5 * ss[t]
+                ge = (ks[t] + k_east[t]) * (half * s_east[t])
+                gw = (ks[t] + k_west[t]) * (half * s_west[t])
+                gn = (ks[t] + kap[t, block(at, 1)]) * (half * mask[level, t, block(at, 1)])
+                gs = (ks[t] + kap[t, block(at, -1)]) * (half * mask[level, t, block(at, -1)])
+                g_mid[level, t, block(at)] = 1.0 - ((ge + gw) + (gn + gs))
+                g_east[level, t, block(at)] = ge
+                g_west[level, t, block(at)] = gw
+                g_north[level, t, block(at)] = gn
 
     @pl.loop(0, levels)
     def _(level):
-        for depth in range(4):
-            advance(level, LEAD - TAIL + STEP * depth, depth)
+        for turn, depth in enumerate((0, 1, 2, 2)):
+            advance(level, LEAD - TAIL + STEP * turn, depth)
 
     def diffuse_chunk(k, level, into):
         @pl.loop(0, per_chunk // STEP)
         def _(j):
             o = k * per_chunk + j * STEP
 
-            def emit(finals):
-                for i in range(STEP):
-                    acc = weight[level, plain(o + i)] * finals[0][i][:, 0:cols]
-                    acc = acc + weight[levels + level, plain(o + i)] * finals[1][i][:, 0:cols]
-                    into[k, plain(j * STEP + i)] = acc
+            def emit(i, finals):
+                for t in range(tiles):
+                    span = slice(t * LANES, (t + 1) * LANES)
+                    acc = weight[level, plain(o + i), span] * finals[t]
+                    acc = acc + weight[levels + level, plain(o + i), span] * finals[tiles + t]
+                    into[k, plain(j * STEP + i), span] = acc
 
             advance(level, o + LEAD, 3, emit)
 
@@ -326,8 +350,11 @@
 
         @pl.loop(0, per_chunk)
         def _(j):
-            sea_here = mask[core, block(k * per_chunk + j), 0:cols]
-            total[k, plain(j)] = (pair[k, plain(j)] + pair_in[k, plain(j)]) * sea_here
+            for t in range(tiles):
+                span = slice(t * LANES, (t + 1) * LANES)
+                total[k, plain(j), span] = (
+                    pair[k, plain(j), span] + pair_in[k, plain(j), span]
+                ) * mask[core, t, block(k * per_chunk + j)]
 
         send_total(k).start()
         store_total(k).start()
@@ -347,15 +374,15 @@
     members, levels, rows, cols = control.shape
     fields = members * levels
     chunks = rows // CHUNK
-    wide = cols + 128
+    span = cols // LANES + 1
     tall = rows + 8 * (PAD + TAIL)
     items = fields + 1 + levels
     count = lax.axis_size("lon")
     f32 = jnp.float32
     any_spec = pl.BlockSpec(memory_space=pl.ANY)
     chunk_buf = pltpu.VMEM((chunks, CHUNK, cols), f32)
-    full = pltpu.VMEM((fields, tall, wide), f32)
-    by_level = pltpu.VMEM((levels, tall, wide), f32)
+    full = pltpu.VMEM((fields, span, tall, LANES), f32)
+    by_level = pltpu.VMEM((levels, span, tall, LANES), f32)
     packed = pltpu.VMEM((2, rows // 4, 128), f32)
     dma = pltpu.SemaphoreType.DMA
     return pl.pallas_call(
@@ -366,16 +393,15 @@
         scratch_shapes=[
             full, full, full,
             pltpu.VMEM((fields, rows, cols), f32),
-            pltpu.VMEM((tall, wide), f32),
+            pltpu.VMEM((span, tall, LANES), f32),
             by_level,
             pltpu.VMEM((levels, rows, cols), jnp.int32),
-            by_level, by_level,
-            pltpu.VMEM((levels, members, PASSES, 8, wide), f32),
+            by_level, by_level, by_level, by_level,
             packed, packed,
             pltpu.VMEM((items, 8, cols), f32),
             pltpu.VMEM((count - 1, items, 8, cols), f32),
             chunk_buf, chunk_buf, chunk_buf, chunk_buf, chunk_buf,
-            dma((4,)), dma((2,)), dma((2,)), dma((3,)), dma((3,)),
+            dma((2 * span,)), dma((2,)), dma((2,)), dma((3,)), dma((3,)),
             dma((count - 1,)), dma((count - 1,)),
             dma((chunks,)), dma((chunks,)), dma((chunks,)), dma((chunks,)),
             dma((chunks,)), dma((chunks,)), dma((chunks,)),

time: 83.2 us -> 64.3 us (0.77)
  Pallas kernels: 78.8 us -> 59.9 us
    pallas_call x1, Pallas kernels: 78.8 us -> 59.9 us  [per_device(): pl.pallas_call(kernel, out_shape=jax.ShapeDtypeStruct((levels, rows, cols...]
where the time goes in v2:
time: 64.3 us; the launch traced here: 64.2 us
  Pallas kernels  59.9 us (93%)
  local copies, waits for them, and re-layouts  4.24 us (7%)
    pallas_call x1, Pallas kernels, per_device(): pl.pallas_call(kernel, out_shape=jax.ShapeDtypeStruct((levels, rows, cols...  59.9 us
    unnamed x1, local copies, waits for them, and re-layouts  3.05 us

profile of v2, /device:TPU:0, one launch (start us, length us, event | category | flops | bytes accessed | tf_op | source)
XLA Modules:
  0.0 64.2 jit_solution(348147007662522009)
XLA Ops:
  0.0 1.2 %slice.3.pivot = s32[1]{0:T(128)} slice(s32[1024]{0:T(1024)} %param.9), slice={[0:1]} | slice | bytes 8 | tf_op jit(solution)/shard_map/slice | solution.py:420
  1.2 59.9 %shard_map.55 = f32[2,1024,256]{2,1,0:T(8,128)} custom-call(f32[4,1024,256]{2,1,0:T(8,128)} %bitcast.2, f32[4,1024,256]{2,1,0:T(8,128)} %bitcast.3, f32[1024,256]{1,0:T(8,128)} %kappa.1, s32[2,1024,256]{2,1,0:T(8,128)} %sea.1, s32[1]{0:T(128)} %slice.3.pivot), custom_call_target="tpu_custom_call" | custom-call | flops 41943040 | bytes 16777216 | tf_op jit(solution)/shard_map/pallas_call | solution.py:388
  61.1 3.0 %copy.7 = f32[2,1024,256]{2,1,0:T(8,128)} copy(f32[2,1024,256]{2,1,0:T(8,128)} %shard_map.55) | data formatting | bytes 4194304

commit v3 on v2

--- a/solution.py
+++ b/solution.py
@@ -55,7 +55,7 @@
             pltpu.make_async_copy(control.at[:, :, span], field.at[:, t, body_rows], in_sem.at[2 + 2 * t]),
             pltpu.make_async_copy(kappa.at[:, span], kap.at[t, body_rows], in_sem.at[3 + 2 * t]),
         ]
-    for copy in loads:
+    for copy in loads[:1] + loads[2:]:
         copy.start()
 
     barrier = pltpu.get_barrier_semaphore()
@@ -97,12 +97,17 @@
     left = 0
     right = tiles - 1
 
-    @pl.loop(0, quarter)
-    def _(b):
+    loads[1].start()
+    part_blocks = quarter // 2
+    starts = (0, 1, 2, 7), (3, 4, 5, 6)
+
+    def pack_part(h):
+      @pl.loop(0, part_blocks)
+      def _(b):
         west = jnp.zeros((8, 128), jnp.float32)
         east = jnp.zeros((8, 128), jnp.float32)
         for g in range(groups):
-            idx = g * quarter + b
+            idx = starts[h][g] * part_blocks + b
             for lev in range(levels):
                 for t in range(tiles):
                     span = slice(t * LANES, (t + 1) * LANES)
@@ -120,24 +125,31 @@
                     lo = pltpu.roll(lo, slot, 1)
                 west = jnp.where(here, lo, west)
                 east = jnp.where(here, pltpu.roll(hi, slot + PASSES, 1), east)
-        pack[0, plain(b)] = west
-        pack[1, plain(b)] = east
-
+        pack[0, plain(h * part_blocks + b)] = west
+        pack[1, plain(h * part_blocks + b)] = east
+
+    pack_part(0)
+    pl.semaphore_wait(barrier, len(peers))
+
+    def side_copy(way, h, peer):
+        span = pl.ds(h * part_blocks * 8, part_blocks * 8)
+        sem = 2 * h + way
+        return pltpu.make_async_remote_copy(
+            src_ref=pack.at[way, span], dst_ref=pack_in.at[way, span], send_sem=side_send.at[sem],
+            recv_sem=side_recv.at[sem], device_id=peer, device_id_type=MESH,
+        )
+
+    halves = [[side_copy(0, h, west_peer), side_copy(1, h, east_peer)] for h in range(2)]
+    sides = halves[0] + halves[1]
+    for copy in halves[0]:
+        copy.start()
+    pack_part(1)
+    for copy in halves[1]:
+        copy.start()
     for item in range(items):
         for t in range(tiles):
             top[item, :, t * LANES : (t + 1) * LANES] = source(item, blocks - 1, t)
 
-    pl.semaphore_wait(barrier, len(peers))
-
-    def side_copy(way, peer):
-        return pltpu.make_async_remote_copy(
-            src_ref=pack.at[way], dst_ref=pack_in.at[way], send_sem=side_send.at[way],
-            recv_sem=side_recv.at[way], device_id=peer, device_id_type=MESH,
-        )
-
-    sides = [side_copy(0, west_peer), side_copy(1, east_peer)]
-    for copy in sides:
-        copy.start()
     gathers = [
         pltpu.make_async_remote_copy(
             src_ref=top, dst_ref=top_in.at[d - 1], send_sem=top_send.at[d - 1],
@@ -147,20 +159,23 @@
     ]
     for copy in gathers:
         copy.start()
-    for copy in sides:
+
+    def unpack_part(h):
+      for copy in halves[h]:
         copy.wait_recv()
 
-    @pl.loop(0, quarter)
-    def _(b):
-        from_east = pack_in[0, plain(b)]
-        from_west = pack_in[1, plain(b)]
+      @pl.loop(0, part_blocks)
+      def _(b):
+        from_east = pack_in[0, plain(h * part_blocks + b)]
+        from_west = pack_in[1, plain(h * part_blocks + b)]
         for g in range(groups):
             for item in range(items):
                 slot = slot_of(item, g)
                 near = pltpu.roll(from_east, 128 - slot, 1) if slot else from_east
                 far = pltpu.roll(from_west, 128 - slot - PASSES, 1)
-                store(item, g * quarter + b, tiles, jnp.where(lane < 64, near, far))
-
+                store(item, starts[h][g] * part_blocks + b, tiles, jnp.where(lane < 64, near, far))
+
+    unpack_part(0)
     rim_from = block((blocks - 1) * (1 - lat))
     rim_to = block(lat * (blocks + 1) - 1)
     rims = [
@@ -231,9 +246,10 @@
 
     every = range(tiles + 1)
 
-    def advance(level, a, depth, emit=None):
+    def advance(level, a, depth, emit=None, put=None):
         for p in range(depth - 1, -1, -1):
             origin = (field, once, again)[p]
+            made = []
             for i in range(STEP):
                 at = a - 5 * p + i
                 used = range(tiles) if p == 2 else every
@@ -257,11 +273,18 @@
                             gn * origin[n, t, block(at, 1)] + gs * origin[n, t, block(at, -1)]
                         )
                         if p < 2:
-                            (once, again)[p][n, t, block(at)] = value
+                            made.append((n, t, at, value))
                         else:
                             finals.append(value)
                 if p == 2:
-                    emit(i, finals)
+                    made.append((i, emit(i, finals)))
+            for entry in made:
+                if p == 2:
+                    put(*entry)
+                else:
+                    n, t, at, value = entry
+                    (once, again)[p][n, t, block(at)] = value
+        made = []
         for i in range(STEP):
             at = a + STEP + i
             ks = [kap[t, block(at)] for t in every]
@@ -274,10 +297,12 @@
                 gw = (ks[t] + k_west[t]) * (half * s_west[t])
                 gn = (ks[t] + kap[t, block(at, 1)]) * (half * mask[level, t, block(at, 1)])
                 gs = (ks[t] + kap[t, block(at, -1)]) * (half * mask[level, t, block(at, -1)])
-                g_mid[level, t, block(at)] = 1.0 - ((ge + gw) + (gn + gs))
-                g_east[level, t, block(at)] = ge
-                g_west[level, t, block(at)] = gw
-                g_north[level, t, block(at)] = gn
+                made.append((t, at, 1.0 - ((ge + gw) + (gn + gs)), ge, gw, gn))
+        for t, at, gm, ge, gw, gn in made:
+            g_mid[level, t, block(at)] = gm
+            g_east[level, t, block(at)] = ge
+            g_west[level, t, block(at)] = gw
+            g_north[level, t, block(at)] = gn
 
     @pl.loop(0, levels)
     def _(level):
@@ -290,13 +315,18 @@
             o = k * per_chunk + j * STEP
 
             def emit(i, finals):
+                sums = []
                 for t in range(tiles):
                     span = slice(t * LANES, (t + 1) * LANES)
                     acc = weight[level, plain(o + i), span] * finals[t]
-                    acc = acc + weight[levels + level, plain(o + i), span] * finals[tiles + t]
-                    into[k, plain(j * STEP + i), span] = acc
-
-            advance(level, o + LEAD, 3, emit)
+                    sums.append(acc + weight[levels + level, plain(o + i), span] * finals[tiles + t])
+                return sums
+
+            def put(i, sums):
+                for t in range(tiles):
+                    into[k, plain(j * STEP + i), t * LANES : (t + 1) * LANES] = sums[t]
+
+            advance(level, o + LEAD, 3, emit, put)
 
     def send_part(k):
         return pltpu.make_async_remote_copy(
@@ -324,6 +354,10 @@
 
     @pl.loop(0, chunks)
     def _(k):
+        @pl.when(k == 2)
+        def _():
+            unpack_part(1)
+
         @pl.when(k == chunks - 2)
         def _():
             for copy in gathers:
@@ -401,7 +435,7 @@
             pltpu.VMEM((items, 8, cols), f32),
             pltpu.VMEM((count - 1, items, 8, cols), f32),
             chunk_buf, chunk_buf, chunk_buf, chunk_buf, chunk_buf,
-            dma((2 * span,)), dma((2,)), dma((2,)), dma((3,)), dma((3,)),
+            dma((2 * span,)), dma((4,)), dma((4,)), dma((3,)), dma((3,)),
             dma((count - 1,)), dma((count - 1,)),
             dma((chunks,)), dma((chunks,)), dma((chunks,)), dma((chunks,)),
             dma((chunks,)), dma((chunks,)), dma((chunks,)),
@@ -417,7 +451,7 @@
         perturb.reshape(fields, rows, cols),
         diffusivity,
         sea_mask,
-        fold_partner[:1],
+        fold_partner,
     )
 
 

time: 64.3 us -> 56.3 us (0.88)
  Pallas kernels: 59.9 us -> 53 us
  local copies, waits for them, and re-layouts: 4.24 us -> 3.05 us
    pallas_call x1, Pallas kernels: 59.9 us -> 53 us  [per_device(): pl.pallas_call(kernel, out_shape=jax.ShapeDtypeStruct((levels, rows, cols...]
    slice x1 -> x0, local copies, waits for them, and re-layouts: 1.2 us -> none  [per_device(): fold_partner[:1]]
where the time goes in v3:
time: 56.3 us; the launch traced here: 56.1 us
  Pallas kernels  53 us (94%)
  local copies, waits for them, and re-layouts  3.05 us (5%)
    pallas_call x1, Pallas kernels, per_device(): pl.pallas_call(kernel, out_shape=jax.ShapeDtypeStruct((levels, rows, cols...  53 us
    unnamed x1, local copies, waits for them, and re-layouts  3.05 us

profile of v3, /device:TPU:0, one launch (start us, length us, event | category | flops | bytes accessed | tf_op | source)
XLA Modules:
  0.0 56.1 jit_solution(12043166895444154829)
XLA Ops:
  0.0 53.0 %shard_map.55 = f32[2,1024,256]{2,1,0:T(8,128)} custom-call(f32[4,1024,256]{2,1,0:T(8,128)} %bitcast.2, f32[4,1024,256]{2,1,0:T(8,128)} %bitcast.3, f32[1024,256]{1,0:T(8,128)} %kappa.1, s32[2,1024,256]{2,1,0:T(8,128)} %sea.1, s32[1024]{0:T(1024)} %pivot.1), custom_call_target="tpu_custom_call" | custom-call | flops 41943040 | bytes 16777216 | tf_op jit(solution)/shard_map/pallas_call | solution.py:422
  53.0 3.0 %copy.7 = f32[2,1024,256]{2,1,0:T(8,128)} copy(f32[2,1024,256]{2,1,0:T(8,128)} %shard_map.55) | data formatting | bytes 4194304
